TPU v7x, 512 devices: a whole 4x8x8 slice. The times are simulated.
512 devices in a mesh: noise: 16 (over z_lo, x), dp: 32 (over z_hi, y, core).
Axes of the slice: x: 4, y: 8, z: 8 (z_hi: 2, z_lo: 4; z = z_hi * 4 + z_lo), core: 2. Of those that a mesh axis runs over, the one named last changes fastest.
Arguments:
- noise_latents: bfloat16 [2048, 65536], P('noise', 'dp'), as said below
- data_latents: bfloat16 [2048, 65536], P('noise', 'dp'), as said below
Outputs:
- targets: bfloat16 [2048, 65536], P('noise', 'dp')
- noise_potential: float32 [2048], P('noise')
- data_potential: float32 [2048], P('dp')
Inputs may be any that keep to these rules, and one draw needn't show every extreme that they name: `noise_latents`: any finite values. `data_latents`: any finite values.
All inputs are finite; a program needn't handle non-finite values.
Results may differ from a plain program's by a relative error of at most 0.002.
Values may be sent and summed in bfloat16 or wider, within the bound.
No kernel may reach another device: no remote copies, remote signals or barrier semaphores. Data moves between devices by JAX's collectives and lax.ppermute only.
A program may use at most 64 MiB of HBM per device.

v0:
```python
import functools
import math

import jax
import jax.numpy as jnp
from jax import lax
from jax.experimental import pallas as pl
from jax.experimental.pallas import tpu as pltpu
from jax.sharding import Mesh
from jax.sharding import PartitionSpec as P

F = 65536
ITERS = 4
eps = 0.01

NOISE = ("zl", "x")
PLANE = ("zh", "y")
DP = ("zh", "y", "c")
LANES = 128
BLOCKS = 4
CHUNK = 512
VMEM = pl.BlockSpec(memory_space=pltpu.VMEM)
SMEM = pl.BlockSpec(memory_space=pltpu.SMEM)
ANY = pl.BlockSpec(memory_space=pl.ANY)
f32 = jnp.float32


def params(mib):
    return pltpu.CompilerParams(vmem_limit_bytes=mib << 20)


def square_sums(ref):
    total = jnp.zeros((ref.shape[0], LANES), f32)
    for start in range(0, ref.shape[1], LANES):
        part = ref[:, start : start + LANES].astype(f32)
        total += part * part
    return jnp.sum(total, axis=1, keepdims=True)


def tile_kernel(place, *refs):
    noise, data = refs[:BLOCKS], refs[BLOCKS : BLOCKS + 6]
    sent, kept, whole, tall, wide, tall_sem, wide_sem, whole_sem = refs[BLOCKS + 6 :]
    rows = noise[0].shape[0]
    sub = kept.shape[2]

    def load_noise(k):
        start = pl.multiple_of(lax.rem(place[0] + BLOCKS - k, BLOCKS) * rows, rows)
        return pltpu.make_async_copy(noise[k], tall.at[pl.ds(start, rows)], tall_sem.at[k])

    def load_data(ref, b):
        start = pl.multiple_of(b * rows, rows)
        return pltpu.make_async_copy(ref, wide.at[pl.ds(start, rows)], wide_sem.at[b])

    for ref, step in [(data[k], step) for k, step in enumerate((0, -1, 1, -2, 2, 3))] + [(data[5], -3)]:
        block = place[1] + step

        @pl.when((block >= 0) & (block < BLOCKS))
        def _():
            load_data(ref, block).start()

    for k in range(BLOCKS):
        load_noise(k).start()
    for b in range(BLOCKS):
        load_data(data[0], b).wait()
    store = pltpu.make_async_copy(wide, whole, whole_sem)
    store.start()

    for k in range(BLOCKS):
        load_noise(k).wait()
    noise_sq = square_sums(tall)
    half_rows = BLOCKS // 2 * rows
    for out, half in ((sent, 1 - place[2]), (kept, place[2])):
        block = wide.at[pl.ds(pl.multiple_of(half * half_rows, half_rows), half_rows)]
        data_sq = jnp.broadcast_to(square_sums(block), (half_rows, LANES)).T[0:1]
        inner = lax.dot_general(tall[...], block[...], (((1,), (1,)), ((), ())), preferred_element_type=f32)
        value = noise_sq + data_sq - 2.0 * inner
        for slot in range(BLOCKS):
            out[:, slot] = value[slot * rows : (slot + 1) * rows].reshape(rows // sub, sub, half_rows)
    store.wait()


def tile(place, noise, data, plane):
    rows, feats = data[0].shape
    dtype = data[0].dtype
    out = jax.ShapeDtypeStruct((plane, BLOCKS, rows // plane, BLOCKS // 2 * rows), f32)
    return pl.pallas_call(
        tile_kernel,
        out_shape=(out, out, jax.ShapeDtypeStruct((BLOCKS * rows, feats), dtype)),
        in_specs=[SMEM] + [ANY] * (BLOCKS + 6),
        out_specs=(VMEM, VMEM, ANY),
        scratch_shapes=[
            pltpu.VMEM((BLOCKS * rows, feats), dtype),
            pltpu.VMEM((BLOCKS * rows, feats), dtype),
            pltpu.SemaphoreType.DMA((BLOCKS,)),
            pltpu.SemaphoreType.DMA((BLOCKS,)),
            pltpu.SemaphoreType.DMA,
        ],
        compiler_params=params(56),
    )(place, *noise, *data)


def half_steps(cost, data_pot, log_a, local):
    blocks, rows, lanes = cost.shape

    def shifted(b):
        return -cost[b] if data_pot is None else data_pot[b : b + 1] - cost[b]

    peak = shifted(0)
    for b in range(1, blocks):
        peak = jnp.maximum(peak, shifted(b))
    peak = jnp.max(peak, axis=1, keepdims=True)
    total = jnp.exp(shifted(0) - peak)
    for b in range(1, blocks):
        total += jnp.exp(shifted(b) - peak)
    noise_pot = log_a - (peak + jnp.log(jnp.sum(total, axis=1, keepdims=True)))
    for b in range(blocks):
        value = noise_pot - cost[b]
        top = jnp.max(value, axis=0, keepdims=True)
        local[0, b : b + 1, :] = top + jnp.log(jnp.sum(jnp.exp(value - top), axis=0, keepdims=True))
    for k in range(1, local.shape[0]):
        local[k] = local[0]
    return noise_pot


def merge(everyone, log_b):
    peak = everyone[0]
    for k in range(1, everyone.shape[0]):
        peak = jnp.maximum(peak, everyone[k])
    total = jnp.exp(everyone[0] - peak)
    for k in range(1, everyone.shape[0]):
        total += jnp.exp(everyone[k] - peak)
    return log_b - (peak + jnp.log(total))


def first_kernel(log_a, place, mine, other, cost, local):
    xs, rows, width = mine.shape
    per_half = width // LANES
    for ref, half in ((mine, place[2]), (other, 1 - place[2])):
        for b in range(xs):
            for q in range(per_half):
                cost[b * BLOCKS + half * per_half + q] = ref[b, :, q * LANES : (q + 1) * LANES]
    half_steps(cost, None, log_a, local)


def middle_kernel(log_a, log_b, cost, everyone, local, noise_pot):
    noise_pot[...] = half_steps(cost, merge(everyone, log_b), log_a, local)


def last_kernel(log_b, place, cost, everyone, noise_pot, whole, targets, noise_out, data_out, pots, plan, data, sems):
    blocks, rows, lanes = cost.shape
    loads = []
    for n in range(targets.shape[1] // CHUNK):
        cols = pl.ds(n * CHUNK, CHUNK)
        loads.append(pltpu.make_async_copy(whole.at[:, cols], data.at[:, cols], sems.at[n]))
        loads[-1].start()

    pots[...] = merge(everyone, log_b)
    scaled = noise_pot[...]
    total = jnp.zeros((rows, lanes), f32)
    for b in range(blocks):
        entry = jnp.exp(scaled + pots[b : b + 1] - cost[b]).astype(jnp.bfloat16)
        total += entry.astype(f32)
        plan[:, b * lanes : (b + 1) * lanes] = entry
    mass = jnp.sum(total, axis=1, keepdims=True)
    noise_out[...] = jnp.broadcast_to(scaled * eps, (rows, lanes)).T[0:1]
    size = data_out.shape[1]
    row = pots[pl.ds(place[3], 1)] * eps
    mine = row[:, :size]
    for k in range(1, lanes // size):
        mine = jnp.where(place[4] == k, row[:, k * size : (k + 1) * size], mine)
    data_out[...] = mine

    for n, load in enumerate(loads):
        load.wait()
        cols = slice(n * CHUNK, (n + 1) * CHUNK)
        moved = jnp.dot(plan[...], data[:, cols], preferred_element_type=f32)
        targets[:, cols] = (moved / mass).astype(jnp.bfloat16)


def shards(noise_latents, data_latents):
    rows, feats = noise_latents.shape
    zl, x, zh, y, c = (lax.axis_size(a) for a in ("zl", "x", "zh", "y", "c"))
    plane = zh * y
    peers = zl * x
    total = peers * rows
    core, xi, zi = (lax.axis_index(a) for a in ("c", "x", "zl"))
    swap = [(0, 1), (1, 0)]

    owner = (lax.axis_index("zh") * y + lax.axis_index("y")) * c + core
    size = total // (plane * c)
    parts = rows // size
    block = owner // parts
    place = jnp.stack([xi, zi, core, (block % x) * zl + block // x, owner % parts])

    def send(value, axis, pairs):
        return lax.ppermute(value, axis, pairs)

    def turn(value, steps):
        return send(value, "x", [(i, (i + steps) % x) for i in range(x)])

    ups = [(i, i + 1) for i in range(zl - 1)]
    downs = [(i + 1, i) for i in range(zl - 1)]
    up, down = send(data_latents, "zl", ups), send(data_latents, "zl", downs)
    ends = send(data_latents, "zl", [(0, zl - 1), (zl - 1, 0)])
    noise = [noise_latents] + [turn(noise_latents, k) for k in range(1, x - 1)]
    up2, down2 = send(up, "zl", ups[1:]), send(down, "zl", downs[:-1])
    later, *_ = lax.optimization_barrier((noise_latents, up, down))
    noise.append(turn(later, x - 1))
    data = [data_latents, up, down, up2, down2, ends]

    sent, kept, whole = tile(place, noise, data, plane)
    came = lax.ppermute(sent, "c", swap)
    data_all = lax.all_gather(whole, "x").reshape(total, feats)
    pieces = lax.all_to_all(kept + came, PLANE, 0, 0, tiled=True)
    piece = jnp.sum(pieces, axis=0) / F / eps

    sub, half = piece.shape[1:]
    copies = jnp.broadcast_to(piece[:, None], (x, plane, sub, half)).reshape(x * plane, sub, half)
    mine = lax.all_to_all(copies, ("x",) + PLANE, 0, 0, tiled=True).reshape(x, rows, half)
    other = lax.ppermute(mine, "c", swap)

    log_a = log_b = -math.log(total)
    blocks = total // LANES
    exchanged = jax.ShapeDtypeStruct((peers, blocks, LANES), f32)
    column = jax.ShapeDtypeStruct((rows, 1), f32)
    cost, local = pl.pallas_call(
        functools.partial(first_kernel, log_a),
        out_shape=(jax.ShapeDtypeStruct((blocks, rows, LANES), f32), exchanged),
        in_specs=[SMEM, VMEM, VMEM],
        out_specs=(VMEM, VMEM),
        compiler_params=params(8),
    )(place, mine, other)
    for step in range(1, ITERS):
        everyone = lax.all_to_all(local, NOISE, 0, 0, tiled=True)
        local, noise_pot = pl.pallas_call(
            functools.partial(middle_kernel, log_a, log_b),
            out_shape=(exchanged, column),
            in_specs=[VMEM, VMEM],
            out_specs=(VMEM, VMEM),
            compiler_params=params(8),
        )(cost, everyone)
    everyone = lax.all_to_all(local, NOISE, 0, 0, tiled=True)

    targets, noise_out, data_out = pl.pallas_call(
        functools.partial(last_kernel, log_b),
        out_shape=(
            jax.ShapeDtypeStruct((rows, feats), jnp.bfloat16),
            jax.ShapeDtypeStruct((1, rows), f32),
            jax.ShapeDtypeStruct((1, size), f32),
        ),
        in_specs=[SMEM, VMEM, VMEM, VMEM] + [ANY],
        out_specs=(VMEM,) * 3,
        scratch_shapes=[
            pltpu.VMEM((blocks, LANES), f32),
            pltpu.VMEM((rows, total), jnp.bfloat16),
            pltpu.VMEM((total, feats), jnp.bfloat16),
            pltpu.SemaphoreType.DMA((feats // CHUNK,)),
        ],
        compiler_params=params(53),
    )(place, cost, everyone, noise_pot, data_all)
    return targets, noise_out[0], data_out[0]


def solution(mesh):
    fine = Mesh(mesh.devices.reshape(4, 4, 2, 8, 2), ("zl", "x", "zh", "y", "c"))
    placed = (P(NOISE, DP), P(NOISE, DP))
    return jax.shard_map(
        shards,
        mesh=fine,
        in_specs=placed,
        out_specs=(P(NOISE, DP), P(NOISE), P(DP)),
        check_vma=False,
    )
```

profile of v0, /device:TPU:8, one launch (start us, length us, event | category | flops | bytes accessed | tf_op | source)
XLA Modules:
  0.0 193.7 jit_solution(8857218715335836069)
XLA Ops:
  7.2 0.0 all-gather.3.cloned.1.call-start
  7.2 1.3 collective-permute-start.3
  8.5 4.9 %collective-permute-start.2 = (bf16[128,2048]{1,0:T(8,128)(2,1)}, bf16[128,2048]{1,0:T(8,128)(2,1)S(1)}, u32[]{:S(2)}, u32[]{:S(2)}) collective-permute-start(bf16[128,2048]{1,0:T(8,128)(2,1)} %refs_4_.1), channel_id=1, source_target_pairs={{0,128},{128,256},{256,384},{1,129},{129,257},{257,385},{2,130},{1... | collective-permute-start | bytes 1572872 | tf_op jit(solution)/shard_map/ppermute | solution.py:196
  13.5 4.9 %collective-permute-start.1 = (bf16[128,2048]{1,0:T(8,128)(2,1)}, bf16[128,2048]{1,0:T(8,128)(2,1)S(1)}, u32[]{:S(2)}, u32[]{:S(2)}) collective-permute-start(bf16[128,2048]{1,0:T(8,128)(2,1)} %refs_0_.1), channel_id=1, source_target_pairs={{0,64},{32,96},{64,0},{96,32},{1,65},{33,97},{65,1},{97,33},{2,66}... | collective-permute-start | bytes 1572872 | tf_op jit(solution)/shard_map/ppermute | solution.py:196
  18.4 2.5 %collective-permute-start = (bf16[128,2048]{1,0:T(8,128)(2,1)}, bf16[128,2048]{1,0:T(8,128)(2,1)S(1)}, u32[]{:S(2)}, u32[]{:S(2)}) collective-permute-start(bf16[128,2048]{1,0:T(8,128)(2,1)} %refs_0_.1), channel_id=1, source_target_pairs={{0,32},{32,64},{64,96},{96,0},{1,33},{33,65},{65,97},{97,1},{2,34}... | collective-permute-start | bytes 1572872 | tf_op jit(solution)/shard_map/ppermute | solution.py:196
  20.9 4.6 %collective-permute-start.7 = (bf16[128,2048]{1,0:T(8,128)(2,1)}, bf16[128,2048]{1,0:T(8,128)(2,1)S(1)}, u32[]{:S(2)}, u32[]{:S(2)}) collective-permute-start(bf16[128,2048]{1,0:T(8,128)(2,1)} %refs_4_.1), channel_id=1, source_target_pairs={{0,384},{384,0},{1,385},{385,1},{2,386},{386,2},{3,387},{387,3},{4... | collective-permute-start | bytes 1572872 | tf_op jit(solution)/shard_map/ppermute | solution.py:196
  25.5 0.0 collective-permute-done.3.refs_6_
  25.5 0.0 copy-start.2
  25.5 0.0 collective-permute-done.2.refs_5_
  25.5 0.0 copy-start.3
  25.5 4.6 %collective-permute-start.4 = (bf16[128,2048]{1,0:T(8,128)(2,1)}, bf16[128,2048]{1,0:T(8,128)(2,1)S(1)}, u32[]{:S(2)}, u32[]{:S(2)}) collective-permute-start(bf16[128,2048]{1,0:T(8,128)(2,1)} %refs_0_.1), channel_id=1, source_target_pairs={{0,96},{32,0},{64,32},{96,64},{1,97},{33,1},{65,33},{97,65},{2,98}... | collective-permute-start | bytes 1572872 | tf_op jit(solution)/shard_map/ppermute | solution.py:196
  30.1 1.3 collective-permute-start.6
  31.4 0.6 collective-permute-done.1.refs_2_
  32.0 0.0 copy-start.4
  32.0 1.5 collective-permute-start.5
  33.4 0.6 stack.23.place
  34.0 0.0 copy-start.1
  34.0 7.6 %collective-permute-done.refs_1_ = bf16[128,2048]{1,0:T(8,128)(2,1)S(1)} collective-permute-done((bf16[128,2048]{1,0:T(8,128)(2,1)}, bf16[128,2048]{1,0:T(8,128)(2,1)S(1)}, u32[]{:S(2)}, u32[]{:S(2)}) %collective-permute-start) | collective-permute-done | bytes 524320 | tf_op jit(solution)/shard_map/ppermute | solution.py:196
  41.7 0.0 copy-start.5
  41.7 0.0 collective-permute-done.7.refs_9_
  41.7 0.0 copy-start.6
  41.7 11.4 %collective-permute-done.6.refs_8_ = bf16[128,2048]{1,0:T(8,128)(2,1)} collective-permute-done((bf16[128,2048]{1,0:T(8,128)(2,1)S(1)}, bf16[128,2048]{1,0:T(8,128)(2,1)}, u32[]{:S(2)}, u32[]{:S(2)}) %collective-permute-start.6) | collective-permute-done | bytes 524320 | tf_op jit(solution)/shard_map/ppermute | solution.py:196
  53.1 0.0 collective-permute-done.4.refs_3_
  53.1 0.0 copy-start.7
  53.1 0.0 collective-permute-done.5.refs_7_
  53.1 0.0 copy-done.2
  53.1 0.0 copy-done.3
  53.1 0.0 copy-done.4
  53.1 0.0 copy-done.5
  53.1 0.0 copy-done.6
  53.1 0.7 copy-done.7
  53.9 5.8 %shard_map.49 = (f32[16,4,8,256]{3,2,1,0:T(8,128)}, f32[16,4,8,256]{3,2,1,0:T(8,128)}, bf16[512,2048]{1,0:T(8,128)(2,1)}) custom-call(s32[5]{0:T(128)} %stack.23.place, bf16[128,2048]{1,0:T(8,128)(2,1)} %refs_0_.1, bf16[128,2048]{1,0:T(8,128)(2,1)} %copy-done.5, bf16[128,2048]{1,0:T(8,128)(2,1)} %copy-done.4, bf16[128,2048]{1,0:T(8,128)(2,1)} %copy-done.7, ...), custom_call_target="tpu_custom_call" | custom-call | tf_op jit(solution)/shard_map/pallas_call | solution.py:86
  59.7 0.0 all-gather.3.cloned.1.call-update
  59.7 1.9 collective-permute-start.8
  61.6 2.1 %collective-permute-done.8 = f32[16,4,8,256]{3,2,1,0:T(8,128)S(1)} collective-permute-done((f32[16,4,8,256]{3,2,1,0:T(8,128)}, f32[16,4,8,256]{3,2,1,0:T(8,128)S(1)}, u32[]{:S(2)}, u32[]{:S(2)}) %collective-permute-start.8) | collective-permute-done | bytes 524320 | tf_op jit(solution)/shard_map/ppermute | solution.py:212
  63.7 1.1 add.26
  64.8 29.9 %all_to_all.30 = f32[16,4,8,256]{3,2,1,0:T(8,128)S(1)} all-to-all(f32[16,4,8,256]{3,2,1,0:T(8,128)S(1)} %add.26), channel_id=1, replica_groups=mesh['zl'=4,'x'=4,'zh'=2,'y'=8,'c'=2] {'zh','y'}, dimensions={0} | all-to-all | bytes 1048576 | tf_op jit(solution)/shard_map/all_to_all | solution.py:214
  94.8 30.5 %all_to_all.31 = f32[64,8,256]{2,1,0:T(8,128)S(1)} all-to-all(f32[64,8,256]{2,1,0:T(8,128)S(1)} %bitcast.11), channel_id=1, replica_groups=mesh['zl'=4,'x'=4,'zh'=2,'y'=8,'c'=2] {'x','zh','y'}, dimensions={0} | all-to-all | bytes 1048576 | tf_op jit(solution)/shard_map/all_to_all | solution.py:219
  125.3 1.9 collective-permute-start.9
  127.2 1.9 collective-permute-done.9.other
  129.1 0.0 copy-done.1
  129.1 1.2 shard_map.50
  130.3 0.0 copy-start
  130.3 12.7 %all_to_all.32.everyone = f32[16,16,128]{2,1,0:T(8,128)S(1)} all-to-all(f32[16,16,128]{2,1,0:T(8,128)S(1)} %get-tuple-element.20), channel_id=1, replica_groups=mesh['zl'=4,'x'=4,'zh'=2,'y'=8,'c'=2] {'zl','x'}, dimensions={0} | all-to-all | bytes 262144 | tf_op jit(solution)/shard_map/all_to_all | solution.py:234
  143.0 1.2 shard_map.51
  144.2 11.8 %all_to_all.33.everyone = f32[16,16,128]{2,1,0:T(8,128)S(1)} all-to-all(f32[16,16,128]{2,1,0:T(8,128)S(1)} %get-tuple-element.21), channel_id=1, replica_groups=mesh['zl'=4,'x'=4,'zh'=2,'y'=8,'c'=2] {'zl','x'}, dimensions={0} | all-to-all | bytes 262144 | tf_op jit(solution)/shard_map/all_to_all | solution.py:234
  156.0 1.2 shard_map.52
  157.2 11.5 %all_to_all.34.everyone = f32[16,16,128]{2,1,0:T(8,128)S(1)} all-to-all(f32[16,16,128]{2,1,0:T(8,128)S(1)} %get-tuple-element.22), channel_id=1, replica_groups=mesh['zl'=4,'x'=4,'zh'=2,'y'=8,'c'=2] {'zl','x'}, dimensions={0} | all-to-all | bytes 262144 | tf_op jit(solution)/shard_map/all_to_all | solution.py:234
  168.7 0.6 shard_map.53
  169.3 11.5 %all_to_all.35.everyone = f32[16,16,128]{2,1,0:T(8,128)S(1)} all-to-all(f32[16,16,128]{2,1,0:T(8,128)S(1)} %get-tuple-element.23), channel_id=1, replica_groups=mesh['zl'=4,'x'=4,'zh'=2,'y'=8,'c'=2] {'zl','x'}, dimensions={0} | all-to-all | bytes 262144 | tf_op jit(solution)/shard_map/all_to_all | solution.py:242
  180.8 0.0 all-gather.3.cloned.1.call-done.whole
  180.8 0.0 copy-done
  180.8 6.0 %shard_map.54 = (bf16[128,2048]{1,0:T(8,128)(2,1)}, f32[1,128]{1,0:T(1,128)}, f32[1,64]{1,0:T(1,128)}) custom-call(s32[5]{0:T(128)S(1)} %copy-done.1, f32[16,128,128]{2,1,0:T(8,128)} %copy-done, f32[16,16,128]{2,1,0:T(8,128)S(1)} %all_to_all.35.everyone, f32[128,1]{1,0:T(8,128)S(1)} %get-tuple-element.24.noise_pot, ...), custom_call_target="tpu_custom_call" | custom-call | tf_op jit(solution)/shard_map/pallas_call | solution.py:244
  (3 shorter events, 0.1 us)
Async XLA Ops:
  7.2 173.7 %all-gather.3.cloned.1.call-start = ((), (), s32[]{:S(2)}) async-start(), calls=%async_computation.6 | async-start | bytes 10485760 | tf_op jit(solution)/shard_map/all_gather | solution.py:213
  7.2 18.3 %collective-permute-start.3 = (bf16[128,2048]{1,0:T(8,128)(2,1)}, bf16[128,2048]{1,0:T(8,128)(2,1)S(1)}, u32[]{:S(2)}, u32[]{:S(2)}) collective-permute-start(bf16[128,2048]{1,0:T(8,128)(2,1)} %refs_4_.1), channel_id=1, source_target_pairs={{128,0},{256,128},{384,256},{129,1},{257,129},{385,257},{130,2},{2... | collective-permute-start | bytes 1572872 | tf_op jit(solution)/shard_map/ppermute | solution.py:196
  8.5 17.0 %collective-permute-start.2 = (bf16[128,2048]{1,0:T(8,128)(2,1)}, bf16[128,2048]{1,0:T(8,128)(2,1)S(1)}, u32[]{:S(2)}, u32[]{:S(2)}) collective-permute-start(bf16[128,2048]{1,0:T(8,128)(2,1)} %refs_4_.1), channel_id=1, source_target_pairs={{0,128},{128,256},{256,384},{1,129},{129,257},{257,385},{2,130},{1... | collective-permute-start | bytes 1572872 | tf_op jit(solution)/shard_map/ppermute | solution.py:196
  13.5 18.5 %collective-permute-start.1 = (bf16[128,2048]{1,0:T(8,128)(2,1)}, bf16[128,2048]{1,0:T(8,128)(2,1)S(1)}, u32[]{:S(2)}, u32[]{:S(2)}) collective-permute-start(bf16[128,2048]{1,0:T(8,128)(2,1)} %refs_0_.1), channel_id=1, source_target_pairs={{0,64},{32,96},{64,0},{96,32},{1,65},{33,97},{65,1},{97,33},{2,66}... | collective-permute-start | bytes 1572872 | tf_op jit(solution)/shard_map/ppermute | solution.py:196
  18.4 23.3 %collective-permute-start = (bf16[128,2048]{1,0:T(8,128)(2,1)}, bf16[128,2048]{1,0:T(8,128)(2,1)S(1)}, u32[]{:S(2)}, u32[]{:S(2)}) collective-permute-start(bf16[128,2048]{1,0:T(8,128)(2,1)} %refs_0_.1), channel_id=1, source_target_pairs={{0,32},{32,64},{64,96},{96,0},{1,33},{33,65},{65,97},{97,1},{2,34}... | collective-permute-start | bytes 1572872 | tf_op jit(solution)/shard_map/ppermute | solution.py:196
  20.9 20.8 %collective-permute-start.7 = (bf16[128,2048]{1,0:T(8,128)(2,1)}, bf16[128,2048]{1,0:T(8,128)(2,1)S(1)}, u32[]{:S(2)}, u32[]{:S(2)}) collective-permute-start(bf16[128,2048]{1,0:T(8,128)(2,1)} %refs_4_.1), channel_id=1, source_target_pairs={{0,384},{384,0},{1,385},{385,1},{2,386},{386,2},{3,387},{387,3},{4... | collective-permute-start | bytes 1572872 | tf_op jit(solution)/shard_map/ppermute | solution.py:196
  25.5 27.6 %copy-start.2 = (bf16[128,2048]{1,0:T(8,128)(2,1)}, bf16[128,2048]{1,0:T(8,128)(2,1)S(1)}, u32[]{:S(2)}) copy-start(bf16[128,2048]{1,0:T(8,128)(2,1)S(1)} %collective-permute-done.3.refs_6_) | copy-start | bytes 1572868
  25.5 27.6 %copy-start.3 = (bf16[128,2048]{1,0:T(8,128)(2,1)}, bf16[128,2048]{1,0:T(8,128)(2,1)S(1)}, u32[]{:S(2)}) copy-start(bf16[128,2048]{1,0:T(8,128)(2,1)S(1)} %collective-permute-done.2.refs_5_) | copy-start | bytes 1572868
  25.5 27.6 %collective-permute-start.4 = (bf16[128,2048]{1,0:T(8,128)(2,1)}, bf16[128,2048]{1,0:T(8,128)(2,1)S(1)}, u32[]{:S(2)}, u32[]{:S(2)}) collective-permute-start(bf16[128,2048]{1,0:T(8,128)(2,1)} %refs_0_.1), channel_id=1, source_target_pairs={{0,96},{32,0},{64,32},{96,64},{1,97},{33,1},{65,33},{97,65},{2,98}... | collective-permute-start | bytes 1572872 | tf_op jit(solution)/shard_map/ppermute | solution.py:196
  30.1 23.0 %collective-permute-start.6 = (bf16[128,2048]{1,0:T(8,128)(2,1)S(1)}, bf16[128,2048]{1,0:T(8,128)(2,1)}, u32[]{:S(2)}, u32[]{:S(2)}) collective-permute-start(bf16[128,2048]{1,0:T(8,128)(2,1)S(1)} %collective-permute-done.3.refs_6_), channel_id=1, source_target_pairs={{128,0},{256,128},{129,1},{257,129},{130,2},{258,130},{131,3},{259... | collective-permute-start | bytes 1572872 | tf_op jit(solution)/shard_map/ppermute | solution.py:196
  32.0 21.2 %copy-start.4 = (bf16[128,2048]{1,0:T(8,128)(2,1)}, bf16[128,2048]{1,0:T(8,128)(2,1)S(1)}, u32[]{:S(2)}) copy-start(bf16[128,2048]{1,0:T(8,128)(2,1)S(1)} %collective-permute-done.1.refs_2_) | copy-start | bytes 1572868
  32.0 21.1 %collective-permute-start.5 = (bf16[128,2048]{1,0:T(8,128)(2,1)S(1)}, bf16[128,2048]{1,0:T(8,128)(2,1)}, u32[]{:S(2)}, u32[]{:S(2)}) collective-permute-start(bf16[128,2048]{1,0:T(8,128)(2,1)S(1)} %collective-permute-done.2.refs_5_), channel_id=1, source_target_pairs={{128,256},{256,384},{129,257},{257,385},{130,258},{258,386},{131,2... | collective-permute-start | bytes 1572872 | tf_op jit(solution)/shard_map/ppermute | solution.py:196
  34.0 95.1 %copy-start.1 = (s32[5]{0:T(128)S(1)}, s32[5]{0:T(128)}, u32[]{:S(2)}) copy-start(s32[5]{0:T(128)} %stack.23.place) | copy-start | bytes 64
  41.7 11.4 %copy-start.5 = (bf16[128,2048]{1,0:T(8,128)(2,1)}, bf16[128,2048]{1,0:T(8,128)(2,1)S(1)}, u32[]{:S(2)}) copy-start(bf16[128,2048]{1,0:T(8,128)(2,1)S(1)} %collective-permute-done.refs_1_) | copy-start | bytes 1572868
  41.7 11.4 %copy-start.6 = (bf16[128,2048]{1,0:T(8,128)(2,1)}, bf16[128,2048]{1,0:T(8,128)(2,1)S(1)}, u32[]{:S(2)}) copy-start(bf16[128,2048]{1,0:T(8,128)(2,1)S(1)} %collective-permute-done.7.refs_9_) | copy-start | bytes 1572868
  53.1 0.8 copy-start.7
  59.7 4.0 %collective-permute-start.8 = (f32[16,4,8,256]{3,2,1,0:T(8,128)}, f32[16,4,8,256]{3,2,1,0:T(8,128)S(1)}, u32[]{:S(2)}, u32[]{:S(2)}) collective-permute-start(f32[16,4,8,256]{3,2,1,0:T(8,128)} %get-tuple-element.18), channel_id=1, source_target_pairs={{0,1},{1,0},{2,3},{3,2},{4,5},{5,4},{6,7},{7,6},{8,9},{9,8},{10,11... | collective-permute-start | bytes 1572872 | tf_op jit(solution)/shard_map/ppermute | solution.py:212
  125.3 3.8 %collective-permute-start.9 = (f32[4,128,256]{2,1,0:T(8,128)S(1)}, f32[4,128,256]{2,1,0:T(8,128)S(1)}, u32[]{:S(2)}, u32[]{:S(2)}) collective-permute-start(f32[4,128,256]{2,1,0:T(8,128)S(1)} %bitcast.9), channel_id=1, source_target_pairs={{0,1},{1,0},{2,3},{3,2},{4,5},{5,4},{6,7},{7,6},{8,9},{9,8},{10,11... | collective-permute-start | bytes 1572872 | tf_op jit(solution)/shard_map/ppermute | solution.py:220
  130.3 50.5 %copy-start = (f32[16,128,128]{2,1,0:T(8,128)}, f32[16,128,128]{2,1,0:T(8,128)S(1)}, u32[]{:S(2)}) copy-start(f32[16,128,128]{2,1,0:T(8,128)S(1)} %get-tuple-element.19.cost) | copy-start | bytes 3145732
Sparse Core Ops, SparseCore 0:
  59.8 96.2 all-gather.2
where the time goes:
time: 194 us
  blocking collectives  108 us (56%)
  starting transfers between devices  29.4 us (15%)
  waiting for transfers between devices  23.6 us (12%)
  Pallas kernels  16 us (8%)
  between operations  14.2 us (7%)
    all_to_all x4, blocking collectives, shards(): everyone = lax.all_to_all(local, NOISE, 0, 0, tiled=True)  47.5 us
    all_to_all x1, blocking collectives, shards(): lax.all_to_all(copies, ('x',) + PLANE, 0, 0, tiled=True)  30.5 us
    all_to_all x1, blocking collectives, shards(): pieces = lax.all_to_all(kept + came, PLANE, 0, 0, tiled=True)  29.9 us
    ppermute x8, starting transfers between devices, send(): return lax.ppermute(value, axis, pairs)  25.5 us
    ppermute x8, waiting for transfers between devices, send(): return lax.ppermute(value, axis, pairs)  19.6 us
    pallas_call x1, Pallas kernels, shards(): pl.pallas_call(functools.partial(last_kernel, log_b), out_shape=(jax.Shap...  6.04 us
    pallas_call x1, Pallas kernels, tile(): pl.pallas_call(tile_kernel, out_shape=(out, out, jax.ShapeDtypeStruct((BL...  5.77 us
  transfers between devices with their start and end apart: 11, of which 5 were waited for; matrix products, arithmetic and copies ran while one was open for 1% of the time, Pallas kernels for 2%

commit v1 on v0

--- a/solution.py
+++ b/solution.py
@@ -142,8 +142,10 @@
     half_steps(cost, None, log_a, local)
 
 
-def middle_kernel(log_a, log_b, cost, everyone, local, noise_pot):
-    noise_pot[...] = half_steps(cost, merge(everyone, log_b), log_a, local)
+def middle_kernel(log_a, log_b, cost, everyone, local, *noise_out):
+    noise_pot = half_steps(cost, merge(everyone, log_b), log_a, local)
+    for ref in noise_out:
+        ref[...] = noise_pot
 
 
 def last_kernel(log_b, place, cost, everyone, noise_pot, whole, targets, noise_out, data_out, pots, plan, data, sems):
@@ -231,15 +233,16 @@
         compiler_params=params(8),
     )(place, mine, other)
     for step in range(1, ITERS):
-        everyone = lax.all_to_all(local, NOISE, 0, 0, tiled=True)
-        local, noise_pot = pl.pallas_call(
+        everyone = lax.all_to_all(local, ("x", "zl"), 0, 0, tiled=True)
+        shapes = (exchanged, column) if step == ITERS - 1 else (exchanged,)
+        local, *noise_pot = pl.pallas_call(
             functools.partial(middle_kernel, log_a, log_b),
-            out_shape=(exchanged, column),
+            out_shape=shapes,
             in_specs=[VMEM, VMEM],
-            out_specs=(VMEM, VMEM),
+            out_specs=(VMEM,) * len(shapes),
             compiler_params=params(8),
         )(cost, everyone)
-    everyone = lax.all_to_all(local, NOISE, 0, 0, tiled=True)
+    everyone = lax.all_to_all(local, ("x", "zl"), 0, 0, tiled=True)
 
     targets, noise_out, data_out = pl.pallas_call(
         functools.partial(last_kernel, log_b),
@@ -248,7 +251,7 @@
             jax.ShapeDtypeStruct((1, rows), f32),
             jax.ShapeDtypeStruct((1, size), f32),
         ),
-        in_specs=[SMEM, VMEM, VMEM, VMEM] + [ANY],
+        in_specs=[SMEM, VMEM, VMEM, VMEM, ANY],
         out_specs=(VMEM,) * 3,
         scratch_shapes=[
             pltpu.VMEM((blocks, LANES), f32),
@@ -257,7 +260,7 @@
             pltpu.SemaphoreType.DMA((feats // CHUNK,)),
         ],
         compiler_params=params(53),
-    )(place, cost, everyone, noise_pot, data_all)
+    )(place, cost, everyone, *noise_pot, data_all)
     return targets, noise_out[0], data_out[0]
 
 

time: 194 us -> 192 us (0.990)
  blocking collectives: 108 us -> 106 us
where the time goes in v1:
time: 192 us; the launch traced here: 191 us
  blocking collectives  106 us (55%)
  starting transfers between devices  29.4 us (15%)
  waiting for transfers between devices  23.6 us (12%)
  Pallas kernels  14.8 us (8%)
  between operations  14.2 us (7%)
    all_to_all x4, blocking collectives, shards(): everyone = lax.all_to_all(local, ('x', 'zl'), 0, 0, tiled=True)  46 us
    all_to_all x1, blocking collectives, shards(): lax.all_to_all(copies, ('x',) + PLANE, 0, 0, tiled=True)  30.5 us
    all_to_all x1, blocking collectives, shards(): pieces = lax.all_to_all(kept + came, PLANE, 0, 0, tiled=True)  29.9 us
    ppermute x8, starting transfers between devices, send(): return lax.ppermute(value, axis, pairs)  25.5 us
    ppermute x8, waiting for transfers between devices, send(): return lax.ppermute(value, axis, pairs)  19.7 us
    pallas_call x1, Pallas kernels, shards(): pl.pallas_call(functools.partial(last_kernel, log_b), out_shape=(jax.Shap...  6.03 us
    pallas_call x1, Pallas kernels, tile(): pl.pallas_call(tile_kernel, out_shape=(out, out, jax.ShapeDtypeStruct((BL...  5.76 us
  transfers between devices with their start and end apart: 11, of which 5 were waited for; matrix products, arithmetic and copies ran while one was open for 1% of the time, Pallas kernels for 2%

profile of v1, /device:TPU:8, one launch (start us, length us, event | category | flops | bytes accessed | tf_op | source)
XLA Modules:
  0.0 191.1 jit_solution(397139975327889923)
XLA Ops:
  7.2 0.0 all-gather.3.cloned.1.call-start
  7.2 1.3 collective-permute-start.3
  8.5 4.9 %collective-permute-start.2 = (bf16[128,2048]{1,0:T(8,128)(2,1)}, bf16[128,2048]{1,0:T(8,128)(2,1)S(1)}, u32[]{:S(2)}, u32[]{:S(2)}) collective-permute-start(bf16[128,2048]{1,0:T(8,128)(2,1)} %refs_4_.1), channel_id=1, source_target_pairs={{0,128},{128,256},{256,384},{1,129},{129,257},{257,385},{2,130},{1... | collective-permute-start | bytes 1572872 | tf_op jit(solution)/shard_map/ppermute | solution.py:198
  13.5 4.9 %collective-permute-start.1 = (bf16[128,2048]{1,0:T(8,128)(2,1)}, bf16[128,2048]{1,0:T(8,128)(2,1)S(1)}, u32[]{:S(2)}, u32[]{:S(2)}) collective-permute-start(bf16[128,2048]{1,0:T(8,128)(2,1)} %refs_0_.1), channel_id=1, source_target_pairs={{0,64},{32,96},{64,0},{96,32},{1,65},{33,97},{65,1},{97,33},{2,66}... | collective-permute-start | bytes 1572872 | tf_op jit(solution)/shard_map/ppermute | solution.py:198
  18.4 2.5 %collective-permute-start = (bf16[128,2048]{1,0:T(8,128)(2,1)}, bf16[128,2048]{1,0:T(8,128)(2,1)S(1)}, u32[]{:S(2)}, u32[]{:S(2)}) collective-permute-start(bf16[128,2048]{1,0:T(8,128)(2,1)} %refs_0_.1), channel_id=1, source_target_pairs={{0,32},{32,64},{64,96},{96,0},{1,33},{33,65},{65,97},{97,1},{2,34}... | collective-permute-start | bytes 1572872 | tf_op jit(solution)/shard_map/ppermute | solution.py:198
  20.9 4.6 %collective-permute-start.7 = (bf16[128,2048]{1,0:T(8,128)(2,1)}, bf16[128,2048]{1,0:T(8,128)(2,1)S(1)}, u32[]{:S(2)}, u32[]{:S(2)}) collective-permute-start(bf16[128,2048]{1,0:T(8,128)(2,1)} %refs_4_.1), channel_id=1, source_target_pairs={{0,384},{384,0},{1,385},{385,1},{2,386},{386,2},{3,387},{387,3},{4... | collective-permute-start | bytes 1572872 | tf_op jit(solution)/shard_map/ppermute | solution.py:198
  25.5 0.0 collective-permute-done.3.refs_6_
  25.5 0.0 copy-start.2
  25.5 0.0 collective-permute-done.2.refs_5_
  25.5 0.0 copy-start.3
  25.5 4.6 %collective-permute-start.4 = (bf16[128,2048]{1,0:T(8,128)(2,1)}, bf16[128,2048]{1,0:T(8,128)(2,1)S(1)}, u32[]{:S(2)}, u32[]{:S(2)}) collective-permute-start(bf16[128,2048]{1,0:T(8,128)(2,1)} %refs_0_.1), channel_id=1, source_target_pairs={{0,96},{32,0},{64,32},{96,64},{1,97},{33,1},{65,33},{97,65},{2,98}... | collective-permute-start | bytes 1572872 | tf_op jit(solution)/shard_map/ppermute | solution.py:198
  30.1 1.3 collective-permute-start.6
  31.4 0.6 collective-permute-done.1.refs_2_
  32.0 0.0 copy-start.4
  32.0 1.5 collective-permute-start.5
  33.4 0.6 stack.23.place
  34.0 0.0 copy-start.1
  34.0 7.7 %collective-permute-done.refs_1_ = bf16[128,2048]{1,0:T(8,128)(2,1)S(1)} collective-permute-done((bf16[128,2048]{1,0:T(8,128)(2,1)}, bf16[128,2048]{1,0:T(8,128)(2,1)S(1)}, u32[]{:S(2)}, u32[]{:S(2)}) %collective-permute-start) | collective-permute-done | bytes 524320 | tf_op jit(solution)/shard_map/ppermute | solution.py:198
  41.7 0.0 copy-start.5
  41.7 0.0 collective-permute-done.7.refs_9_
  41.7 0.0 copy-start.6
  41.7 11.4 %collective-permute-done.6.refs_8_ = bf16[128,2048]{1,0:T(8,128)(2,1)} collective-permute-done((bf16[128,2048]{1,0:T(8,128)(2,1)S(1)}, bf16[128,2048]{1,0:T(8,128)(2,1)}, u32[]{:S(2)}, u32[]{:S(2)}) %collective-permute-start.6) | collective-permute-done | bytes 524320 | tf_op jit(solution)/shard_map/ppermute | solution.py:198
  53.1 0.0 collective-permute-done.4.refs_3_
  53.1 0.0 copy-start.7
  53.1 0.0 collective-permute-done.5.refs_7_
  53.1 0.0 copy-done.2
  53.1 0.0 copy-done.3
  53.1 0.0 copy-done.4
  53.1 0.0 copy-done.5
  53.1 0.0 copy-done.6
  53.1 0.7 copy-done.7
  53.9 5.8 %shard_map.49 = (f32[16,4,8,256]{3,2,1,0:T(8,128)}, f32[16,4,8,256]{3,2,1,0:T(8,128)}, bf16[512,2048]{1,0:T(8,128)(2,1)}) custom-call(s32[5]{0:T(128)} %stack.23.place, bf16[128,2048]{1,0:T(8,128)(2,1)} %refs_0_.1, bf16[128,2048]{1,0:T(8,128)(2,1)} %copy-done.5, bf16[128,2048]{1,0:T(8,128)(2,1)} %copy-done.4, bf16[128,2048]{1,0:T(8,128)(2,1)} %copy-done.7, ...), custom_call_target="tpu_custom_call" | custom-call | tf_op jit(solution)/shard_map/pallas_call | solution.py:86
  59.7 0.0 all-gather.3.cloned.1.call-update
  59.7 1.9 %collective-permute-start.8 = (f32[16,4,8,256]{3,2,1,0:T(8,128)}, f32[16,4,8,256]{3,2,1,0:T(8,128)S(1)}, u32[]{:S(2)}, u32[]{:S(2)}) collective-permute-start(f32[16,4,8,256]{3,2,1,0:T(8,128)} %get-tuple-element.16), channel_id=1, source_target_pairs={{0,1},{1,0},{2,3},{3,2},{4,5},{5,4},{6,7},{7,6},{8,9},{9,8},{10,11... | collective-permute-start | bytes 1572872 | tf_op jit(solution)/shard_map/ppermute | solution.py:214
  61.6 2.1 %collective-permute-done.8 = f32[16,4,8,256]{3,2,1,0:T(8,128)S(1)} collective-permute-done((f32[16,4,8,256]{3,2,1,0:T(8,128)}, f32[16,4,8,256]{3,2,1,0:T(8,128)S(1)}, u32[]{:S(2)}, u32[]{:S(2)}) %collective-permute-start.8) | collective-permute-done | bytes 524320 | tf_op jit(solution)/shard_map/ppermute | solution.py:214
  63.7 1.1 add.26
  64.8 29.9 %all_to_all.30 = f32[16,4,8,256]{3,2,1,0:T(8,128)S(1)} all-to-all(f32[16,4,8,256]{3,2,1,0:T(8,128)S(1)} %add.26), channel_id=1, replica_groups=mesh['zl'=4,'x'=4,'zh'=2,'y'=8,'c'=2] {'zh','y'}, dimensions={0} | all-to-all | bytes 1048576 | tf_op jit(solution)/shard_map/all_to_all | solution.py:216
  94.8 30.5 %all_to_all.31 = f32[64,8,256]{2,1,0:T(8,128)S(1)} all-to-all(f32[64,8,256]{2,1,0:T(8,128)S(1)} %bitcast.11), channel_id=1, replica_groups=mesh['zl'=4,'x'=4,'zh'=2,'y'=8,'c'=2] {'x','zh','y'}, dimensions={0} | all-to-all | bytes 1048576 | tf_op jit(solution)/shard_map/all_to_all | solution.py:221
  125.3 1.9 collective-permute-start.9
  127.2 1.9 collective-permute-done.9.other
  129.1 0.0 copy-done.1
  129.1 1.2 shard_map.50
  130.3 0.0 copy-start
  130.3 12.2 %all_to_all.32.everyone = f32[16,16,128]{2,1,0:T(8,128)S(1)} all-to-all(f32[16,16,128]{2,1,0:T(8,128)S(1)} %get-tuple-element.18), channel_id=1, replica_groups=mesh['zl'=4,'x'=4,'zh'=2,'y'=8,'c'=2] {'x','zl'}, dimensions={0} | all-to-all | bytes 262144 | tf_op jit(solution)/shard_map/all_to_all | solution.py:236
  142.5 0.6 shard_map.51
  143.1 11.4 %all_to_all.33.everyone = f32[16,16,128]{2,1,0:T(8,128)S(1)} all-to-all(f32[16,16,128]{2,1,0:T(8,128)S(1)} %shard_map.51), channel_id=1, replica_groups=mesh['zl'=4,'x'=4,'zh'=2,'y'=8,'c'=2] {'x','zl'}, dimensions={0} | all-to-all | bytes 262144 | tf_op jit(solution)/shard_map/all_to_all | solution.py:236
  154.5 0.6 shard_map.52
  155.1 11.2 %all_to_all.34.everyone = f32[16,16,128]{2,1,0:T(8,128)S(1)} all-to-all(f32[16,16,128]{2,1,0:T(8,128)S(1)} %shard_map.52), channel_id=1, replica_groups=mesh['zl'=4,'x'=4,'zh'=2,'y'=8,'c'=2] {'x','zl'}, dimensions={0} | all-to-all | bytes 262144 | tf_op jit(solution)/shard_map/all_to_all | solution.py:236
  166.4 0.6 shard_map.53
  167.0 11.2 %all_to_all.35.everyone = f32[16,16,128]{2,1,0:T(8,128)S(1)} all-to-all(f32[16,16,128]{2,1,0:T(8,128)S(1)} %get-tuple-element.19), channel_id=1, replica_groups=mesh['zl'=4,'x'=4,'zh'=2,'y'=8,'c'=2] {'x','zl'}, dimensions={0} | all-to-all | bytes 262144 | tf_op jit(solution)/shard_map/all_to_all | solution.py:245
  178.2 0.0 all-gather.3.cloned.1.call-done.whole
  178.2 0.0 copy-done
  178.2 6.0 %shard_map.54 = (bf16[128,2048]{1,0:T(8,128)(2,1)}, f32[1,128]{1,0:T(1,128)}, f32[1,64]{1,0:T(1,128)}) custom-call(s32[5]{0:T(128)S(1)} %copy-done.1, f32[16,128,128]{2,1,0:T(8,128)} %copy-done, f32[16,16,128]{2,1,0:T(8,128)S(1)} %all_to_all.35.everyone, f32[128,1]{1,0:T(8,128)S(1)} %get-tuple-element.20.noise_pot, ...), custom_call_target="tpu_custom_call" | custom-call | tf_op jit(solution)/shard_map/pallas_call | solution.py:247
  (3 shorter events, 0.1 us)
Async XLA Ops:
  7.2 171.0 %all-gather.3.cloned.1.call-start = ((), (), s32[]{:S(2)}) async-start(), calls=%async_computation.6 | async-start | bytes 10485760 | tf_op jit(solution)/shard_map/all_gather | solution.py:215
  7.2 18.3 %collective-permute-start.3 = (bf16[128,2048]{1,0:T(8,128)(2,1)}, bf16[128,2048]{1,0:T(8,128)(2,1)S(1)}, u32[]{:S(2)}, u32[]{:S(2)}) collective-permute-start(bf16[128,2048]{1,0:T(8,128)(2,1)} %refs_4_.1), channel_id=1, source_target_pairs={{128,0},{256,128},{384,256},{129,1},{257,129},{385,257},{130,2},{2... | collective-permute-start | bytes 1572872 | tf_op jit(solution)/shard_map/ppermute | solution.py:198
  8.5 17.0 %collective-permute-start.2 = (bf16[128,2048]{1,0:T(8,128)(2,1)}, bf16[128,2048]{1,0:T(8,128)(2,1)S(1)}, u32[]{:S(2)}, u32[]{:S(2)}) collective-permute-start(bf16[128,2048]{1,0:T(8,128)(2,1)} %refs_4_.1), channel_id=1, source_target_pairs={{0,128},{128,256},{256,384},{1,129},{129,257},{257,385},{2,130},{1... | collective-permute-start | bytes 1572872 | tf_op jit(solution)/shard_map/ppermute | solution.py:198
  13.5 18.5 %collective-permute-start.1 = (bf16[128,2048]{1,0:T(8,128)(2,1)}, bf16[128,2048]{1,0:T(8,128)(2,1)S(1)}, u32[]{:S(2)}, u32[]{:S(2)}) collective-permute-start(bf16[128,2048]{1,0:T(8,128)(2,1)} %refs_0_.1), channel_id=1, source_target_pairs={{0,64},{32,96},{64,0},{96,32},{1,65},{33,97},{65,1},{97,33},{2,66}... | collective-permute-start | bytes 1572872 | tf_op jit(solution)/shard_map/ppermute | solution.py:198
  18.4 23.3 %collective-permute-start = (bf16[128,2048]{1,0:T(8,128)(2,1)}, bf16[128,2048]{1,0:T(8,128)(2,1)S(1)}, u32[]{:S(2)}, u32[]{:S(2)}) collective-permute-start(bf16[128,2048]{1,0:T(8,128)(2,1)} %refs_0_.1), channel_id=1, source_target_pairs={{0,32},{32,64},{64,96},{96,0},{1,33},{33,65},{65,97},{97,1},{2,34}... | collective-permute-start | bytes 1572872 | tf_op jit(solution)/shard_map/ppermute | solution.py:198
  20.9 20.8 %collective-permute-start.7 = (bf16[128,2048]{1,0:T(8,128)(2,1)}, bf16[128,2048]{1,0:T(8,128)(2,1)S(1)}, u32[]{:S(2)}, u32[]{:S(2)}) collective-permute-start(bf16[128,2048]{1,0:T(8,128)(2,1)} %refs_4_.1), channel_id=1, source_target_pairs={{0,384},{384,0},{1,385},{385,1},{2,386},{386,2},{3,387},{387,3},{4... | collective-permute-start | bytes 1572872 | tf_op jit(solution)/shard_map/ppermute | solution.py:198
  25.5 27.6 %copy-start.2 = (bf16[128,2048]{1,0:T(8,128)(2,1)}, bf16[128,2048]{1,0:T(8,128)(2,1)S(1)}, u32[]{:S(2)}) copy-start(bf16[128,2048]{1,0:T(8,128)(2,1)S(1)} %collective-permute-done.3.refs_6_) | copy-start | bytes 1572868
  25.5 27.6 %copy-start.3 = (bf16[128,2048]{1,0:T(8,128)(2,1)}, bf16[128,2048]{1,0:T(8,128)(2,1)S(1)}, u32[]{:S(2)}) copy-start(bf16[128,2048]{1,0:T(8,128)(2,1)S(1)} %collective-permute-done.2.refs_5_) | copy-start | bytes 1572868
  25.5 27.6 %collective-permute-start.4 = (bf16[128,2048]{1,0:T(8,128)(2,1)}, bf16[128,2048]{1,0:T(8,128)(2,1)S(1)}, u32[]{:S(2)}, u32[]{:S(2)}) collective-permute-start(bf16[128,2048]{1,0:T(8,128)(2,1)} %refs_0_.1), channel_id=1, source_target_pairs={{0,96},{32,0},{64,32},{96,64},{1,97},{33,1},{65,33},{97,65},{2,98}... | collective-permute-start | bytes 1572872 | tf_op jit(solution)/shard_map/ppermute | solution.py:198
  30.1 23.0 %collective-permute-start.6 = (bf16[128,2048]{1,0:T(8,128)(2,1)S(1)}, bf16[128,2048]{1,0:T(8,128)(2,1)}, u32[]{:S(2)}, u32[]{:S(2)}) collective-permute-start(bf16[128,2048]{1,0:T(8,128)(2,1)S(1)} %collective-permute-done.3.refs_6_), channel_id=1, source_target_pairs={{128,0},{256,128},{129,1},{257,129},{130,2},{258,130},{131,3},{259... | collective-permute-start | bytes 1572872 | tf_op jit(solution)/shard_map/ppermute | solution.py:198
  32.0 21.2 %copy-start.4 = (bf16[128,2048]{1,0:T(8,128)(2,1)}, bf16[128,2048]{1,0:T(8,128)(2,1)S(1)}, u32[]{:S(2)}) copy-start(bf16[128,2048]{1,0:T(8,128)(2,1)S(1)} %collective-permute-done.1.refs_2_) | copy-start | bytes 1572868
  32.0 21.1 %collective-permute-start.5 = (bf16[128,2048]{1,0:T(8,128)(2,1)S(1)}, bf16[128,2048]{1,0:T(8,128)(2,1)}, u32[]{:S(2)}, u32[]{:S(2)}) collective-permute-start(bf16[128,2048]{1,0:T(8,128)(2,1)S(1)} %collective-permute-done.2.refs_5_), channel_id=1, source_target_pairs={{128,256},{256,384},{129,257},{257,385},{130,258},{258,386},{131,2... | collective-permute-start | bytes 1572872 | tf_op jit(solution)/shard_map/ppermute | solution.py:198
  34.0 95.1 %copy-start.1 = (s32[5]{0:T(128)S(1)}, s32[5]{0:T(128)}, u32[]{:S(2)}) copy-start(s32[5]{0:T(128)} %stack.23.place) | copy-start | bytes 64
  41.7 11.4 %copy-start.5 = (bf16[128,2048]{1,0:T(8,128)(2,1)}, bf16[128,2048]{1,0:T(8,128)(2,1)S(1)}, u32[]{:S(2)}) copy-start(bf16[128,2048]{1,0:T(8,128)(2,1)S(1)} %collective-permute-done.refs_1_) | copy-start | bytes 1572868
  41.7 11.4 %copy-start.6 = (bf16[128,2048]{1,0:T(8,128)(2,1)}, bf16[128,2048]{1,0:T(8,128)(2,1)S(1)}, u32[]{:S(2)}) copy-start(bf16[128,2048]{1,0:T(8,128)(2,1)S(1)} %collective-permute-done.7.refs_9_) | copy-start | bytes 1572868
  53.1 0.8 copy-start.7
  59.7 4.0 %collective-permute-start.8 = (f32[16,4,8,256]{3,2,1,0:T(8,128)}, f32[16,4,8,256]{3,2,1,0:T(8,128)S(1)}, u32[]{:S(2)}, u32[]{:S(2)}) collective-permute-start(f32[16,4,8,256]{3,2,1,0:T(8,128)} %get-tuple-element.16), channel_id=1, source_target_pairs={{0,1},{1,0},{2,3},{3,2},{4,5},{5,4},{6,7},{7,6},{8,9},{9,8},{10,11... | collective-permute-start | bytes 1572872 | tf_op jit(solution)/shard_map/ppermute | solution.py:214
  125.3 3.8 %collective-permute-start.9 = (f32[4,128,256]{2,1,0:T(8,128)S(1)}, f32[4,128,256]{2,1,0:T(8,128)S(1)}, u32[]{:S(2)}, u32[]{:S(2)}) collective-permute-start(f32[4,128,256]{2,1,0:T(8,128)S(1)} %bitcast.9), channel_id=1, source_target_pairs={{0,1},{1,0},{2,3},{3,2},{4,5},{5,4},{6,7},{7,6},{8,9},{9,8},{10,11... | collective-permute-start | bytes 1572872 | tf_op jit(solution)/shard_map/ppermute | solution.py:222
  130.3 47.9 %copy-start = (f32[16,128,128]{2,1,0:T(8,128)}, f32[16,128,128]{2,1,0:T(8,128)S(1)}, u32[]{:S(2)}) copy-start(f32[16,128,128]{2,1,0:T(8,128)S(1)} %get-tuple-element.17.cost) | copy-start | bytes 3145732
Sparse Core Ops, SparseCore 0:
  59.8 96.2 all-gather.2
